TPU v7x, 32 devices: a whole 2x2x4 slice. The times are simulated.
32 devices in a mesh: dp: 2 (over x), node: 2 (over core), local: 8 (over z, y).
Axes of the slice: x: 2, y: 2, z: 4, core: 2. Of those that a mesh axis runs over, the one named last changes fastest.
Arguments:
- tokens: bfloat16 [4096, 2048], P(('dp', 'node', 'local')), may hold values from -6 to 6
- cotangent: bfloat16 [4096, 2048], P(('dp', 'node', 'local')), may hold values from -4 to 4
- routes: int32 [4096, 8], P(('dp', 'node', 'local')), may hold values from 0 to 15, all different within a row; in each aligned block of 128 rows (0 to 127, 128 to 255, ...) at most 96 rows name the same one
- gates: bfloat16 [4096, 8], P(('dp', 'node', 'local')), may hold values from 0.029907227 to 0.3984375
- w_gate: bfloat16 [16, 2048, 384], P(('node', 'local'), 'dp'), may hold values from -0.125 to 0.125
- w_up: bfloat16 [16, 2048, 384], P(('node', 'local'), 'dp'), may hold values from -0.125 to 0.125
- w_down: bfloat16 [16, 2048, 384], P(('node', 'local'), 'dp'), may hold values from -0.3125 to 0.3125
Outputs:
- input_grad: bfloat16 [4096, 2048], P(('dp', 'node', 'local'))
- gate_grad: bfloat16 [4096, 8], P(('dp', 'node', 'local'))
- gate_weight_grad: float32 [16, 2048, 384], P(('node', 'local'), 'dp')
- up_weight_grad: float32 [16, 2048, 384], P(('node', 'local'), 'dp')
- down_weight_grad: float32 [16, 2048, 384], P(('node', 'local'), 'dp')
Inputs may be any that keep to these rules, and one draw needn't show every extreme that they name: `routes`: each token names 8 different experts. Among the tokens of one device no expert is named more than 96 times, and on some device some expert is named exactly 96 times.
All inputs are finite; a program needn't handle non-finite values.
Results may differ from a plain program's by a relative error of at most 0.0057.
Values may be sent and summed in bfloat16 or wider, within the bound.
A program may use at most 128 MiB of HBM per device.

v0:
```python
import jax
import jax.numpy as jnp
from jax import lax
from jax.sharding import PartitionSpec as P


def expert_rows(rows_x, rows_dy, rows_gate, gate_proj, up_proj, down_proj):
    pre_gate = jnp.dot(rows_x, gate_proj, preferred_element_type=jnp.float32)
    pre_up = jnp.dot(rows_x, up_proj, preferred_element_type=jnp.float32)
    gate_sigmoid = jax.nn.sigmoid(pre_gate)
    activated = pre_gate * gate_sigmoid
    hidden = activated * pre_up
    upstream = jnp.dot(rows_dy, down_proj, preferred_element_type=jnp.float32)
    gate_grad = jnp.sum(upstream * hidden, axis=1).astype(jnp.bfloat16)
    weight = rows_gate.astype(jnp.float32)[:, None]
    scaled_hidden = (weight * hidden).astype(jnp.bfloat16)
    hidden_grad = weight * upstream
    pre_gate_grad = (
        hidden_grad * pre_up * gate_sigmoid * (1.0 + pre_gate * (1.0 - gate_sigmoid))
    ).astype(jnp.bfloat16)
    pre_up_grad = (hidden_grad * activated).astype(jnp.bfloat16)
    over_rows = (((0,), (0,)), ((), ()))
    down_grad = lax.dot_general(
        rows_dy, scaled_hidden, over_rows, preferred_element_type=jnp.float32
    )
    gate_wgrad = lax.dot_general(
        rows_x, pre_gate_grad, over_rows, preferred_element_type=jnp.float32
    )
    up_wgrad = lax.dot_general(rows_x, pre_up_grad, over_rows, preferred_element_type=jnp.float32)
    over_hidden = (((1,), (1,)), ((), ()))
    input_rows = lax.dot_general(
        pre_gate_grad, gate_proj, over_hidden, preferred_element_type=jnp.float32
    )
    input_rows = input_rows + lax.dot_general(
        pre_up_grad, up_proj, over_hidden, preferred_element_type=jnp.float32
    )
    return (input_rows.astype(jnp.bfloat16), gate_grad, gate_wgrad, up_wgrad, down_grad)


def run_tiles(
    packed_x, packed_dy, packed_gate, tile_count, tile_rows, gate_proj, up_proj, down_proj
):
    length, width = packed_x.shape
    hidden_units = gate_proj.shape[1]
    tile_total = length // tile_rows
    tiled = (
        packed_x.reshape(tile_total, tile_rows, width),
        packed_dy.reshape(tile_total, tile_rows, width),
        packed_gate.reshape(tile_total, tile_rows),
        jnp.arange(tile_total, dtype=jnp.int32),
    )

    def work(item):
        return expert_rows(item[0], item[1], item[2], gate_proj, up_proj, down_proj)

    def skip(item):
        return (
            jnp.zeros((tile_rows, width), jnp.bfloat16),
            jnp.zeros((tile_rows,), jnp.bfloat16),
            jnp.zeros((width, hidden_units), jnp.float32),
            jnp.zeros((width, hidden_units), jnp.float32),
            jnp.zeros((width, hidden_units), jnp.float32),
        )

    def one_tile(running, item):
        results = lax.cond(item[3] < tile_count, work, skip, item)
        gate_acc, up_acc, down_acc = running
        return (
            (gate_acc + results[2], up_acc + results[3], down_acc + results[4]),
            (results[0], results[1]),
        )

    start_state = (
        jnp.zeros((width, hidden_units), jnp.float32),
        jnp.zeros((width, hidden_units), jnp.float32),
        jnp.zeros((width, hidden_units), jnp.float32),
    )
    sums, rows_out = lax.scan(one_tile, start_state, tiled)
    return (
        rows_out[0].reshape(length, width),
        rows_out[1].reshape(length),
        sums[0],
        sums[1],
        sums[2],
    )


def local(tokens, cotangent, routes, gates, w_gate, w_up, w_down):
    tokens_dev, top_count = routes.shape
    width = tokens.shape[1]
    groups = lax.axis_size("node")
    members = lax.axis_size("local")
    experts = groups * members
    capacity = min(
        tokens_dev,
        max(3 * tokens_dev * top_count // (2 * experts), tokens_dev * top_count // experts),
    )
    pick_count = tokens_dev * top_count
    slots = experts * capacity
    flat_routes = routes.reshape(pick_count)
    one_hot = (flat_routes[:, None] == jnp.arange(experts, dtype=jnp.int32)[None, :]).astype(
        jnp.int32
    )
    rank = jnp.sum((jnp.cumsum(one_hot, axis=0) - one_hot) * one_hot, axis=1)
    target = flat_routes * capacity + rank
    filler = (
        jnp.full((slots,), -1, jnp.int32).at[target].set(jnp.arange(pick_count, dtype=jnp.int32))
    )
    is_filled = filler >= 0
    safe_pick = jnp.where(is_filled, filler, 0)
    owner_token = safe_pick // top_count
    send_x = jnp.where(is_filled[:, None], tokens[owner_token], jnp.zeros((), tokens.dtype))
    send_dy = jnp.where(is_filled[:, None], cotangent[owner_token], jnp.zeros((), cotangent.dtype))
    send_gate = jnp.where(
        is_filled, gates.reshape(pick_count)[safe_pick], jnp.zeros((), gates.dtype)
    )
    full_weights = (
        lax.all_gather(w_gate, "dp", axis=1, tiled=True),
        lax.all_gather(w_up, "dp", axis=1, tiled=True),
        lax.all_gather(w_down, "dp", axis=1, tiled=True),
    )
    gate_proj = full_weights[0][0]
    up_proj = full_weights[1][0]
    down_proj = full_weights[2][0]
    recv_x, recv_dy, recv_gate = (
        lax.all_to_all(
            send_x.reshape(experts, capacity, width),
            ("node", "local"),
            split_axis=0,
            concat_axis=0,
            tiled=True,
        ),
        lax.all_to_all(
            send_dy.reshape(experts, capacity, width),
            ("node", "local"),
            split_axis=0,
            concat_axis=0,
            tiled=True,
        ),
        lax.all_to_all(
            send_gate.reshape(experts, capacity),
            ("node", "local"),
            split_axis=0,
            concat_axis=0,
            tiled=True,
        ),
    )
    flat_x = recv_x.reshape(slots, width)
    flat_dy = recv_dy.reshape(slots, width)
    flat_gate = recv_gate.reshape(slots)
    tile_rows = min(512, slots)
    length = (slots + tile_rows - 1) // tile_rows * tile_rows
    is_live = flat_gate > 0
    position = jnp.cumsum(is_live.astype(jnp.int32)) - 1
    live_total = jnp.sum(is_live.astype(jnp.int32))
    source = (
        jnp.full((length,), slots, jnp.int32)
        .at[jnp.where(is_live, position, length)]
        .set(jnp.arange(slots, dtype=jnp.int32), mode="drop")
    )
    packed_x = jnp.concatenate([flat_x, jnp.zeros((1, width), flat_x.dtype)])[source]
    packed_dy = jnp.concatenate([flat_dy, jnp.zeros((1, width), flat_dy.dtype)])[source]
    packed_gate = jnp.concatenate([flat_gate, jnp.zeros((1,), flat_gate.dtype)])[source]
    tile_count = (live_total + tile_rows - 1) // tile_rows
    results = run_tiles(
        packed_x, packed_dy, packed_gate, tile_count, tile_rows, gate_proj, up_proj, down_proj
    )
    back_index = jnp.where(is_live, position, length)
    input_rows = jnp.concatenate([results[0], jnp.zeros((1, width), jnp.bfloat16)])[back_index]
    gate_rows = jnp.concatenate([results[1], jnp.zeros((1,), jnp.bfloat16)])[back_index]
    home_x, home_gate = (
        lax.all_to_all(
            input_rows.reshape(experts, capacity, width),
            ("node", "local"),
            split_axis=0,
            concat_axis=0,
            tiled=True,
        ),
        lax.all_to_all(
            gate_rows.reshape(experts, capacity),
            ("node", "local"),
            split_axis=0,
            concat_axis=0,
            tiled=True,
        ),
    )
    per_pick = home_x.reshape(slots, width)[target].reshape(tokens_dev, top_count, width)
    input_grad = jnp.sum(per_pick, axis=1, dtype=jnp.float32).astype(jnp.bfloat16)
    gate_grad = home_gate.reshape(slots)[target].reshape(tokens_dev, top_count)
    summed = (
        lax.psum_scatter(results[2], "dp", scatter_dimension=0, tiled=True),
        lax.psum_scatter(results[3], "dp", scatter_dimension=0, tiled=True),
        lax.psum_scatter(results[4], "dp", scatter_dimension=0, tiled=True),
    )
    return (input_grad, gate_grad, summed[0][None], summed[1][None], summed[2][None])


def solution(mesh):
    placed = (
        P(("dp", "node", "local"), None),
        P(("dp", "node", "local"), None),
        P(("dp", "node", "local"), None),
        P(("dp", "node", "local"), None),
        P(("node", "local"), "dp", None),
        P(("node", "local"), "dp", None),
        P(("node", "local"), "dp", None),
    )
    return jax.shard_map(
        local,
        mesh=mesh,
        in_specs=placed,
        out_specs=(
            P(("dp", "node", "local"), None),
            P(("dp", "node", "local"), None),
            P(("node", "local"), "dp", None),
            P(("node", "local"), "dp", None),
            P(("node", "local"), "dp", None),
        ),
        check_vma=False,
    )
```

profile of v0, /device:TPU:0, one launch (start us, length us, event | category | flops | bytes accessed | tf_op | source)
XLA Modules:
  0.0 673.9 jit_solution(345670667269427332)
XLA Ops:
  8.9 4.5 reduce-window.15
  14.1 4.3 scatter_custom_fusion
  19.4 9.5 %gather_fusion = bf16[1536]{0:T(1024)(128)(2,1)S(1)} fusion(bf16[1024]{0:T(1024)(128)(2,1)S(1)} %reshape.221, s32[2048]{0:T(1024)S(1)} %pad_clamp_fusion.3), kind=kCustom, calls=%fused_computation | custom fusion | bytes 12288 | tf_op jit(solution)/shard_map/gather | solution.py:115
  29.6 7.4 %all-to-all-start = ((bf16[16,1,96]{2,1,0:T(2,128)(2,1)}), bf16[16,1,96]{2,1,0:T(2,128)(2,1)S(1)}, u32[]{:S(2)}, u32[]{:S(2)}) async-start(bf16[16,1,96]{2,1,0:T(2,128)(2,1)} %all_to_all.28), calls=%async_computation | async-start | bytes 16384 | tf_op jit(solution)/shard_map/all_to_all | solution.py:140
  37.1 7.1 %gather_fusion.4 = bf16[1536,2048]{1,0:T(8,128)(2,1)} fusion(bf16[128,2048]{1,0:T(8,128)(2,1)S(1)} %copy-done, s32[2048]{0:T(1024)S(1)} %pad_clamp_fusion.2), kind=kCustom, calls=%fused_computation.4 | custom fusion | bytes 12589056 | tf_op jit(solution)/shard_map/gather | solution.py:113
  44.2 7.0 %gather_fusion.1 = bf16[1536,2048]{1,0:T(8,128)(2,1)} fusion(bf16[128,2048]{1,0:T(8,128)(2,1)S(1)} %copy-done.2, s32[2048]{0:T(1024)S(1)} %pad_clamp_fusion.2), kind=kCustom, calls=%fused_computation.1 | custom fusion | bytes 12589056 | tf_op jit(solution)/shard_map/gather | solution.py:112
  51.2 10.3 %broadcast_select_fusion = (bf16[16,96,2048]{2,1,0:T(8,128)(2,1)}, bf16[16,96,2048]{2,1,0:T(8,128)(2,1)}) fusion(bf16[16,96,2048]{2,1,0:T(8,128)(2,1)} %bitcast.85, pred[16,96]{1,0:T(8,128)(4,1)S(1)} %broadcast_in_dim.91, bf16[16,96,2048]{2,1,0:T(8,128)(2,1)} %bitcast.86), kind=kLoop, calls=%fused_computation.51 | loop fusion | flops 6291456 | bytes 25167360 | tf_op jit(solution)/shard_map/jit(_where)/select_n | solution.py:113
  61.5 145.5 %all_to_all.35 = bf16[16,96,2048]{2,1,0:T(8,128)(2,1)} all-to-all(bf16[16,96,2048]{2,1,0:T(8,128)(2,1)} %get-tuple-element.264), channel_id=1, replica_groups=mesh['dp'=2,'node'=2,'local'=8] {'node','local'}, dimensions={0} | all-to-all | bytes 12582912 | tf_op jit(solution)/shard_map/all_to_all | solution.py:126
  207.0 4.7 all-to-all-start.2
  216.9 6.4 scatter_custom_fusion.1
  223.3 9.5 %gather_fusion.3 = bf16[1536]{0:T(1024)(128)(2,1)S(1)} fusion(bf16[1537]{0:T(1024)(128)(2,1)S(1)} %pad_maximum_fusion.1, s32[2048]{0:T(1024)S(1)} %pad_clamp_fusion.1), kind=kCustom, calls=%fused_computation.3 | custom fusion | bytes 12288 | tf_op jit(solution)/shard_map/gather | solution.py:163
  232.8 6.6 concatenate.15
  239.4 16.3 %gather_fusion.2 = bf16[1536,2048]{1,0:T(8,128)(2,1)} fusion(bf16[1537,2048]{1,0:T(8,128)(2,1)} %concatenate.15, s32[2048]{0:T(1024)S(1)} %pad_clamp_fusion.1), kind=kCustom, calls=%fused_computation.2 | custom fusion | bytes 12589056 | tf_op jit(solution)/shard_map/gather | solution.py:161
  255.6 87.9 %all-to-all-done.2 = bf16[16,96,2048]{2,1,0:T(8,128)(2,1)} async-done(((bf16[16,96,2048]{2,1,0:T(8,128)(2,1)}), bf16[16,96,2048]{2,1,0:T(8,128)(2,1)}, u32[]{:S(2)}, u32[]{:S(2)}) %all-to-all-start.2) | async-done | bytes 6291488 | tf_op jit(solution)/shard_map/all_to_all | solution.py:133
  343.5 6.6 concatenate.17
  350.1 16.3 %gather_fusion.5 = bf16[1536,2048]{1,0:T(8,128)(2,1)} fusion(bf16[1537,2048]{1,0:T(8,128)(2,1)} %concatenate.17, s32[2048]{0:T(1024)S(1)} %pad_clamp_fusion.1), kind=kCustom, calls=%fused_computation.5 | custom fusion | bytes 12589056 | tf_op jit(solution)/shard_map/gather | solution.py:162
  366.5 100.0 %while.19 = (s32[]{:T(128)}, f32[2048,384]{1,0:T(8,128)}, f32[2048,384]{1,0:T(8,128)}, f32[2048,384]{1,0:T(8,128)}, bf16[3,512,2048]{2,1,0:T(8,128)(2,1)}, /*ind...) while((s32[]{:T(128)}, f32[2048,384]{1,0:T(8,128)}, ...), condition=%wide.region_12.13_spmd.clone, body=%wide.region_8.12_spmd.clone.sunk | while | flops 6453985280 | bytes 168048624 | solution.py:78
  367.9 19.4 %conditional.3 = (f32[2048,384]{1,0:T(8,128)}, f32[2048,384]{1,0:T(8,128)}, f32[2048,384]{1,0:T(8,128)}, bf16[1,512,2048]{2,1,0:T(8,128)(2,1)S(1)}, bf16[1,512]{1,0:T(2,128)(2,1)S(1)}) conditional(s32[]{:T(128)} %convert_element_type.89, () %tuple.58, (bf16[3,512,2048]{2,1,0:T(8,128)(2,1)}, s32[]{:T(128)}, bf16[3,512]{1,0:T(4,128)(2,1)S(1)}, ...), branch_computations={%region_9.9_spmd, %region_10.11_spmd} | conditional | flops 6449266688 | bytes 110374096 | solution.py:66
  387.4 6.3 select_add_fusion.6
  399.9 19.4 %conditional.3 = (f32[2048,384]{1,0:T(8,128)}, f32[2048,384]{1,0:T(8,128)}, f32[2048,384]{1,0:T(8,128)}, bf16[1,512,2048]{2,1,0:T(8,128)(2,1)S(1)}, bf16[1,512]{1,0:T(2,128)(2,1)S(1)}) conditional(s32[]{:T(128)} %convert_element_type.89, () %tuple.58, (bf16[3,512,2048]{2,1,0:T(8,128)(2,1)}, s32[]{:T(128)}, bf16[3,512]{1,0:T(4,128)(2,1)S(1)}, ...), branch_computations={%region_9.9_spmd, %region_10.11_spmd} | conditional | flops 6449266688 | bytes 110374096 | solution.py:66
  419.4 8.1 %select_add_fusion.6 = (f32[2048,384]{1,0:T(8,128)}, f32[2048,384]{1,0:T(8,128)}) fusion(f32[2048,384]{1,0:T(8,128)} %get-tuple-element.358, f32[2048,384]{1,0:T(8,128)} %get-tuple-element.393, pred[]{:T(512)S(6)} %compare.10, f32[2048,384]{1,0:T(8,128)} %get-tuple-element.359, f32[2048,384]{1,0:T(8,128)} %get-tuple-element.392), kind=kLoop, calls=%fused_computation.47.clone.1 | loop fusion | flops 3145728 | bytes 18874368 | tf_op jit(solution)/shard_map/while/body/eval_jaxpr/add | solution.py:69
  433.7 19.4 %conditional.3 = (f32[2048,384]{1,0:T(8,128)}, f32[2048,384]{1,0:T(8,128)}, f32[2048,384]{1,0:T(8,128)}, bf16[1,512,2048]{2,1,0:T(8,128)(2,1)S(1)}, bf16[1,512]{1,0:T(2,128)(2,1)S(1)}) conditional(s32[]{:T(128)} %convert_element_type.89, () %tuple.58, (bf16[3,512,2048]{2,1,0:T(8,128)(2,1)}, s32[]{:T(128)}, bf16[3,512]{1,0:T(4,128)(2,1)S(1)}, ...), branch_computations={%region_9.9_spmd, %region_10.11_spmd} | conditional | flops 6449266688 | bytes 110374096 | solution.py:66
  453.2 8.1 %select_add_fusion.6 = (f32[2048,384]{1,0:T(8,128)}, f32[2048,384]{1,0:T(8,128)}) fusion(f32[2048,384]{1,0:T(8,128)} %get-tuple-element.358, f32[2048,384]{1,0:T(8,128)} %get-tuple-element.393, pred[]{:T(512)S(6)} %compare.10, f32[2048,384]{1,0:T(8,128)} %get-tuple-element.359, f32[2048,384]{1,0:T(8,128)} %get-tuple-element.392), kind=kLoop, calls=%fused_computation.47.clone.1 | loop fusion | flops 3145728 | bytes 18874368 | tf_op jit(solution)/shard_map/while/body/eval_jaxpr/add | solution.py:69
  467.2 9.5 %gather_fusion.8 = bf16[1536]{0:T(1024)(128)(2,1)S(1)} fusion(bf16[1537]{0:T(1024)(128)(2,1)S(1)} %pad_maximum_fusion, s32[2048]{0:T(1024)S(1)} %pad_clamp_fusion), kind=kCustom, calls=%fused_computation.8 | custom fusion | bytes 12288 | tf_op jit(solution)/shard_map/gather | solution.py:170
  477.4 9.9 %all-to-all-start.4 = ((bf16[16,1,96]{2,1,0:T(2,128)(2,1)}), bf16[16,1,96]{2,1,0:T(2,128)(2,1)S(1)}, u32[]{:S(2)}, u32[]{:S(2)}) async-start(bf16[16,1,96]{2,1,0:T(2,128)(2,1)} %all_to_all.29), calls=%async_computation.4 | async-start | bytes 16384 | tf_op jit(solution)/shard_map/all_to_all | solution.py:179
  487.3 6.6 concatenate.18
  493.9 16.3 %gather_fusion.6 = bf16[1536,2048]{1,0:T(8,128)(2,1)} fusion(bf16[1537,2048]{1,0:T(8,128)(2,1)} %concatenate.18, s32[2048]{0:T(1024)S(1)} %pad_clamp_fusion), kind=kCustom, calls=%fused_computation.6 | custom fusion | bytes 12589056 | tf_op jit(solution)/shard_map/gather | solution.py:169
  510.2 6.1 all-to-all-start.3
  517.1 6.8 %gather_fusion.9 = bf16[1024]{0:T(1024)(128)(2,1)S(1)} fusion(bf16[1536]{0:T(1024)(128)(2,1)S(1)} %reshape.234, s32[1024]{0:T(1024)S(1)} %broadcast_clamp_fusion), kind=kCustom, calls=%fused_computation.9 | custom fusion | bytes 8192 | tf_op jit(solution)/shard_map/gather | solution.py:189
  524.7 123.6 %all-to-all-done.3 = bf16[16,96,2048]{2,1,0:T(8,128)(2,1)} async-done(((bf16[16,96,2048]{2,1,0:T(8,128)(2,1)}), bf16[16,96,2048]{2,1,0:T(8,128)(2,1)}, u32[]{:S(2)}, u32[]{:S(2)}) %all-to-all-start.3) | async-done | bytes 6291488 | tf_op jit(solution)/shard_map/all_to_all | solution.py:172
  648.3 12.5 %gather_fusion.7 = bf16[1024,2048]{1,0:T(8,128)(2,1)} fusion(bf16[1536,2048]{1,0:T(8,128)(2,1)} %bitcast.19, s32[1024]{0:T(1024)S(1)} %broadcast_clamp_fusion), kind=kCustom, calls=%fused_computation.7 | custom fusion | bytes 8392704 | tf_op jit(solution)/shard_map/gather | solution.py:187
  660.7 5.9 bitcast_reduce_fusion
  (182 shorter events, 86.2 us)
Async XLA Ops:
  7.2 29.9 %copy-start = (bf16[128,2048]{1,0:T(8,128)(2,1)S(1)}, bf16[128,2048]{1,0:T(8,128)(2,1)}, u32[]{:S(2)}) copy-start(bf16[128,2048]{1,0:T(8,128)(2,1)} %param.12) | copy-start | bytes 1572868
  14.1 4.4 copy-start.9
  29.6 31.9 %all-to-all-start = ((bf16[16,1,96]{2,1,0:T(2,128)(2,1)}), bf16[16,1,96]{2,1,0:T(2,128)(2,1)S(1)}, u32[]{:S(2)}, u32[]{:S(2)}) async-start(bf16[16,1,96]{2,1,0:T(2,128)(2,1)} %all_to_all.28), calls=%async_computation | async-start | bytes 16384 | tf_op jit(solution)/shard_map/all_to_all | solution.py:140
  37.1 7.1 %copy-start.2 = (bf16[128,2048]{1,0:T(8,128)(2,1)S(1)}, bf16[128,2048]{1,0:T(8,128)(2,1)}, u32[]{:S(2)}) copy-start(bf16[128,2048]{1,0:T(8,128)(2,1)} %param.11) | copy-start | bytes 1572868
  207.0 136.5 %all-to-all-start.2 = ((bf16[16,96,2048]{2,1,0:T(8,128)(2,1)}), bf16[16,96,2048]{2,1,0:T(8,128)(2,1)}, u32[]{:S(2)}, u32[]{:S(2)}) async-start(bf16[16,96,2048]{2,1,0:T(8,128)(2,1)} %get-tuple-element.263), calls=%async_computation.2 | async-start | bytes 12582912 | tf_op jit(solution)/shard_map/all_to_all | solution.py:133
  211.7 154.8 %all-gather.4.cloned.1.call-start = ((), (), s32[]{:S(2)}) async-start(), calls=%async_computation.8 | async-start | bytes 2359296 | tf_op jit(solution)/shard_map/all_gather | solution.py:120
  212.4 154.0 %all-gather.6.cloned.1.call-start = ((), (), s32[]{:S(2)}) async-start(), calls=%async_computation.9 | async-start | bytes 2359296 | tf_op jit(solution)/shard_map/all_gather | solution.py:119
  213.2 153.3 %all-gather.8.cloned.1.call-start = ((), (), s32[]{:S(2)}) async-start(), calls=%async_computation.10 | async-start | bytes 2359296 | tf_op jit(solution)/shard_map/all_gather | solution.py:118
  213.9 452.7 %reduce-scatter.4.cloned.1.call-start = ((), (), s32[]{:S(2)}) async-start(), calls=%async_computation.11 | async-start | bytes 4718592 | tf_op jit(solution)/shard_map/reduce_scatter | solution.py:191
  367.9 3.3 copy-start.5
  368.0 6.1 copy-start.7
  371.2 2.8 copy-start.11
  374.0 4.1 slice-start
  375.4 2.7 slice-start.1
  387.4 6.3 copy-start.3
  399.9 3.3 copy-start.5
  400.0 6.1 copy-start.7
  403.2 2.8 copy-start.11
  406.0 4.1 slice-start
  407.4 2.7 slice-start.1
  419.4 8.1 %copy-start.3 = (f32[2048,384]{1,0:T(8,128)S(1)}, f32[2048,384]{1,0:T(8,128)}, u32[]{:S(2)}) copy-start(f32[2048,384]{1,0:T(8,128)} %get-tuple-element.391) | copy-start | bytes 9437188 | tf_op jit(solution)/shard_map/while
  433.7 3.3 copy-start.5
  433.7 6.1 copy-start.7
  437.0 2.8 copy-start.11
  439.8 4.1 slice-start
  441.2 2.7 slice-start.1
  453.2 8.1 %copy-start.3 = (f32[2048,384]{1,0:T(8,128)S(1)}, f32[2048,384]{1,0:T(8,128)}, u32[]{:S(2)}) copy-start(f32[2048,384]{1,0:T(8,128)} %get-tuple-element.391) | copy-start | bytes 9437188 | tf_op jit(solution)/shard_map/while
  466.5 200.1 %reduce-scatter.6.cloned.1.call-start = ((), (), s32[]{:S(2)}) async-start(), calls=%async_computation.12 | async-start | bytes 4718592 | tf_op jit(solution)/shard_map/reduce_scatter | solution.py:192
  477.4 32.8 %all-to-all-start.4 = ((bf16[16,1,96]{2,1,0:T(2,128)(2,1)}), bf16[16,1,96]{2,1,0:T(2,128)(2,1)S(1)}, u32[]{:S(2)}, u32[]{:S(2)}) async-start(bf16[16,1,96]{2,1,0:T(2,128)(2,1)} %all_to_all.29), calls=%async_computation.4 | async-start | bytes 16384 | tf_op jit(solution)/shard_map/all_to_all | solution.py:179
  510.2 138.1 %all-to-all-start.3 = ((bf16[16,96,2048]{2,1,0:T(8,128)(2,1)}), bf16[16,96,2048]{2,1,0:T(8,128)(2,1)}, u32[]{:S(2)}, u32[]{:S(2)}) async-start(bf16[16,96,2048]{2,1,0:T(8,128)(2,1)} %bitcast.84), calls=%async_computation.3 | async-start | bytes 12582912 | tf_op jit(solution)/shard_map/all_to_all | solution.py:172
  516.3 150.3 %reduce-scatter.8.cloned.1.call-start = ((), (), s32[]{:S(2)}) async-start(), calls=%async_computation.13 | async-start | bytes 4718592 | tf_op jit(solution)/shard_map/reduce_scatter | solution.py:193
  648.3 18.3 %copy-start.1 = (bf16[128,2048]{1,0:T(8,128)(2,1)S(1)}, bf16[128,2048]{1,0:T(8,128)(2,1)}, u32[]{:S(2)}) copy-start(bf16[128,2048]{1,0:T(8,128)(2,1)} %param.12) | copy-start | bytes 1572868
  (8 other events, 12.5 us)
Sparse Core Ops, SparseCore 0:
  214.1 28.3 all-gather.3
  244.0 27.2 all-gather.5
  272.8 27.1 all-gather.7
  466.7 48.5 reduce-scatter.3
  518.0 43.3 reduce-scatter.5
  564.1 43.3 reduce-scatter.7
where the time goes:
time: 686 us; the launch traced here: 674 us
  waiting for transfers between devices  215 us (31%)
  local copies, waits for them, and re-layouts  155 us (23%)
  blocking collectives  146 us (21%)
  matrix products  57.5 us (8%)
  other arithmetic  54 us (8%)
  starting transfers between devices  28.4 us (4%)
  between operations  15.5 us (2%)
    all_to_all x1, blocking collectives, local(): lax.all_to_all(send_x.reshape(experts, capacity, width), ('node', 'local'...  146 us
    all_to_all x1, waiting for transfers between devices, local(): lax.all_to_all(input_rows.reshape(experts, capacity, width), ('node', 'lo...  124 us
    all_to_all x1, waiting for transfers between devices, local(): lax.all_to_all(send_dy.reshape(experts, capacity, width), ('node', 'local...  87.9 us
    add x3, other arithmetic, one_tile(): down_acc + results[4]  22.4 us
    gather x1, local copies, waits for them, and re-layouts, local(): jnp.concatenate([flat_dy, jnp.zeros((1, width), flat_dy.dtype)])[source]  16.3 us
    gather x1, local copies, waits for them, and re-layouts, local(): jnp.concatenate([results[0], jnp.zeros((1, width), jnp.bfloat16)])  16.3 us
    gather x1, local copies, waits for them, and re-layouts, local(): jnp.concatenate([flat_x, jnp.zeros((1, width), flat_x.dtype)])[source]  16.3 us
  transfers between devices with their start and end apart: 10, of which 2 were waited for; matrix products, arithmetic and copies ran while one was open for 22% of the time, Pallas kernels for 0%

commit v1 on v0

v1 whole, which is shorter than its diff:
```python
import jax
import jax.numpy as jnp
from jax import lax
from jax.sharding import PartitionSpec as P

EXPERT_AXES = ("node", "local")
PIECE_TOKENS = 2048


def local(tokens, cotangent, routes, gates, w_gate, w_up, w_down):
    tokens_dev, width = tokens.shape
    half, units = w_gate.shape[1:]
    members = lax.axis_size("local")
    experts = lax.axis_size("node") * members
    replicas = lax.axis_size("dp")
    expert = lax.axis_index("node") * members + lax.axis_index("local")
    dp = lax.axis_index("dp")

    named = routes[:, :, None] == jnp.arange(experts, dtype=jnp.int32)[None, None, :]
    table = jnp.sum(
        jnp.where(named, gates.astype(jnp.float32)[:, :, None], 0.0), axis=1
    ).astype(jnp.bfloat16)

    w_in = lax.all_gather(
        jnp.concatenate([w_gate[0], w_up[0]], axis=1), "dp", axis=0, tiled=True
    )
    w_out = lax.all_gather(w_down[0], "dp", axis=0, tiled=True)
    mine = jnp.arange(experts, dtype=jnp.int32)[None, :] == expert
    over_rows = (((0,), (0,)), ((), ()))

    def piece(tokens, cotangent, table):
        all_table = lax.all_gather(table, EXPERT_AXES, axis=0, tiled=True)
        x = lax.all_gather(tokens, EXPERT_AXES, axis=0, tiled=True)
        dy = lax.all_gather(cotangent, EXPERT_AXES, axis=0, tiled=True)
        weight = jnp.sum(jnp.where(mine, all_table.astype(jnp.float32), 0.0), axis=1)[:, None]
        pre = jnp.dot(x, w_in, preferred_element_type=jnp.float32)
        upstream = jnp.dot(dy, w_out, preferred_element_type=jnp.float32)
        pre_gate, pre_up = pre[:, :units], pre[:, units:]
        sig = jax.nn.sigmoid(pre_gate)
        activated = pre_gate * sig
        hidden = activated * pre_up
        gate_row = jnp.sum(upstream * hidden, axis=1).astype(jnp.bfloat16)
        scaled_hidden = (weight * hidden).astype(jnp.bfloat16)
        hidden_grad = weight * upstream
        gate_part = hidden_grad * pre_up * sig * (1.0 + pre_gate * (1.0 - sig))
        pre_grad = jnp.concatenate(
            [gate_part.astype(jnp.bfloat16), (hidden_grad * activated).astype(jnp.bfloat16)],
            axis=1,
        )
        rows = lax.dot_general(
            pre_grad, w_in, (((1,), (1,)), ((), ())), preferred_element_type=jnp.float32
        ).astype(jnp.bfloat16)
        input_grad = lax.psum_scatter(rows, EXPERT_AXES, scatter_dimension=0, tiled=True)
        in_grad = lax.dot_general(x, pre_grad, over_rows, preferred_element_type=jnp.float32)
        out_grad = lax.dot_general(
            dy, scaled_hidden, over_rows, preferred_element_type=jnp.float32
        )
        gate_rows = lax.all_gather(gate_row, EXPERT_AXES, axis=0, tiled=True)
        count = tokens.shape[0]
        gate_rows = lax.dynamic_slice_in_dim(
            gate_rows.reshape(experts, experts * count), expert * count, count, axis=1
        )
        return in_grad, out_grad, input_grad, gate_rows

    pieces = max(1, experts * tokens_dev // PIECE_TOKENS)
    if pieces == 1:
        in_grad, out_grad, input_grad, by_expert = piece(tokens, cotangent, table)
    else:

        def step(running, item):
            got = piece(*item)
            return (running[0] + got[0], running[1] + got[1]), got[2:]

        start = (
            jnp.zeros((width, 2 * units), jnp.float32),
            jnp.zeros((width, units), jnp.float32),
        )
        cut = [a.reshape(pieces, -1, a.shape[1]) for a in (tokens, cotangent, table)]
        (in_grad, out_grad), (input_grad, by_expert) = lax.scan(step, start, tuple(cut))
        input_grad = input_grad.reshape(tokens_dev, width)
        by_expert = by_expert.transpose(1, 0, 2).reshape(experts, tokens_dev)

    def own(total):
        return lax.dynamic_slice_in_dim(total, dp * half, half, axis=0)

    def over_replicas(total):
        acc = own(total)
        for shift in range(1, replicas):
            to = lax.rem(dp + shift, replicas)
            part = lax.dynamic_slice_in_dim(total, to * half, half, axis=0)
            pairs = [(i, (i + shift) % replicas) for i in range(replicas)]
            acc = acc + lax.ppermute(part.astype(jnp.bfloat16), "dp", pairs).astype(jnp.float32)
        return acc

    in_sum = over_replicas(in_grad)
    out_sum = over_replicas(out_grad)

    gate_grad = jnp.sum(
        jnp.where(named, by_expert.T.astype(jnp.float32)[:, None, :], 0.0), axis=2
    ).astype(jnp.bfloat16)
    return (
        input_grad,
        gate_grad,
        in_sum[:, :units][None],
        in_sum[:, units:][None],
        out_sum[None],
    )


def solution(mesh):
    rows = P(("dp", "node", "local"), None)
    weights = P(("node", "local"), "dp", None)
    return jax.shard_map(
        local,
        mesh=mesh,
        in_specs=(rows, rows, rows, rows, weights, weights, weights),
        out_specs=(rows, rows, weights, weights, weights),
        check_vma=False,
    )
```

time: 686 us -> 434 us (0.63); the launches traced: 674 us -> 434 us
  local copies, waits for them, and re-layouts: 155 us -> 10 us
  blocking collectives: 146 us -> 60.1 us
  waiting for transfers between devices: 215 us -> 287 us
  other arithmetic: 54 us -> 11.9 us
  starting transfers between devices: 28.4 us -> 2.97 us
  matrix products: 57.5 us -> 47.6 us
    all_gather x3 -> x4, waiting for transfers between devices: 0.01 us -> 215 us  [the longest x1 77.1 us: piece(): x = lax.all_gather(tokens, EXPERT_AXES, axis=0, tiled=True)]
    all_to_all x4 -> x0, waiting for transfers between devices: 211 us -> none  [the longest x1 124 us: local(): lax.all_to_all(input_rows.reshape(experts, capacity, width), ('node', 'lo...]
    all_to_all x1 -> x0, blocking collectives: 146 us -> none  [local(): lax.all_to_all(send_x.reshape(experts, capacity, width), ('node', 'local'...]
    gather x10 -> x0, local copies, waits for them, and re-layouts: 111 us -> none  [the longest x1 16.3 us: local(): jnp.concatenate([flat_dy, jnp.zeros((1, width), flat_dy.dtype)])[source]]
    all_gather x0 -> x2, blocking collectives: none -> 60.1 us  [the longest x1 30.2 us: piece(): gate_rows = lax.all_gather(gate_row, EXPERT_AXES, axis=0, tiled=True)]
    ppermute x0 -> x2, waiting for transfers between devices: none -> 42.4 us  [over_replicas(): lax.ppermute(part.astype(jnp.bfloat16), 'dp', pairs).astype(jnp.float32)]
    all_to_all x4 -> x0, starting transfers between devices: 28.1 us -> none  [the longest x1 9.93 us: local(): lax.all_to_all(gate_rows.reshape(experts, capacity), ('node', 'local'), s...]
    reduce_scatter x3 -> x1, waiting for transfers between devices: 0.01 us -> 27.9 us  [piece(): lax.psum_scatter(rows, EXPERT_AXES, scatter_dimension=0, tiled=True)]
  transfers between devices with their start and end apart: 10 -> 7, of which waited for: 2 -> 6; matrix products, arithmetic and copies ran while one was open for 22% -> 9% of each run, Pallas kernels for 0% -> 0%
where the time goes in v1:
time: 434 us
  waiting for transfers between devices  287 us (66%)
  blocking collectives  60.1 us (14%)
  matrix products  47.6 us (11%)
  between operations  14 us (3%)
  other arithmetic  11.9 us (3%)
  local copies, waits for them, and re-layouts  10 us (2%)
    all_gather x1, waiting for transfers between devices, piece(): x = lax.all_gather(tokens, EXPERT_AXES, axis=0, tiled=True)  77.1 us
    all_gather x1, waiting for transfers between devices, piece(): dy = lax.all_gather(cotangent, EXPERT_AXES, axis=0, tiled=True)  77 us
    all_gather x1, waiting for transfers between devices, local(): lax.all_gather(jnp.concatenate([w_gate[0], w_up[0]], axis=1), 'dp', axis=...  45.7 us
    ppermute x2, waiting for transfers between devices, over_replicas(): lax.ppermute(part.astype(jnp.bfloat16), 'dp', pairs).astype(jnp.float32)  42.4 us
    all_gather x1, blocking collectives, piece(): gate_rows = lax.all_gather(gate_row, EXPERT_AXES, axis=0, tiled=True)  30.2 us
    all_gather x1, blocking collectives, piece(): all_table = lax.all_gather(table, EXPERT_AXES, axis=0, tiled=True)  29.9 us
    reduce_scatter x1, waiting for transfers between devices, piece(): lax.psum_scatter(rows, EXPERT_AXES, scatter_dimension=0, tiled=True)  27.9 us
    all_gather x1, waiting for transfers between devices, local(): w_out = lax.all_gather(w_down[0], 'dp', axis=0, tiled=True)  15.2 us
  transfers between devices with their start and end apart: 7, of which 6 were waited for; matrix products, arithmetic and copies ran while one was open for 9% of the time, Pallas kernels for 0%

profile of v1, /device:TPU:0, one launch (start us, length us, event | category | flops | bytes accessed | tf_op | source)
XLA Modules:
  0.0 434.0 jit_solution(14845641618390944131)
XLA Ops:
  7.2 2.6 pad_maximum_fusion.3
  9.9 0.7 all-gather.10.cloned.1.call-update
  10.7 0.7 all-gather.12.cloned.1.call-update
  11.4 0.5 all-gather.6.cloned.1.call-update
  12.0 45.7 %all-gather.8.cloned.1.call-done = bf16[2048,768]{1,0:T(8,128)(2,1)} async-done(((bf16[1024,768]{1,0:T(8,128)(2,1)}), bf16[2048,768]{1,0:T(8,128)(2,1)}) %all-gather.8.cloned.1.call-update) | async-done | bytes 3145744 | tf_op jit(solution)/shard_map/all_gather | solution.py:24
  57.8 77.1 %all-gather.10.cloned.1.call-done = bf16[2048,2048]{1,0:T(8,128)(2,1)} async-done(((bf16[128,2048]{1,0:T(8,128)(2,1)}), bf16[2048,2048]{1,0:T(8,128)(2,1)}) %all-gather.10.cloned.1.call-update) | async-done | bytes 8388624 | tf_op jit(solution)/shard_map/all_gather | solution.py:33
  134.9 11.8 %convolution_bitcast_fusion = f32[2048,768]{0,1:T(8,128)} fusion(bf16[2048,768]{1,0:T(8,128)(2,1)} %all-gather.8.cloned.1.call-done, bf16[2048,2048]{1,0:T(8,128)(2,1)} %all-gather.10.cloned.1.call-done), kind=kOutput, calls=%fused_computation.1 | convolution fusion | flops 6442450944 | bytes 17825792 | tf_op jit(solution)/shard_map/dot_general | solution.py:36
  146.7 15.2 %all-gather.12.cloned.1.call-done = bf16[1,2048,384]{2,1,0:T(8,128)(2,1)} async-done(((bf16[1,1024,384]{2,1,0:T(8,128)(2,1)}), bf16[1,2048,384]{2,1,0:T(8,128)(2,1)}) %all-gather.12.cloned.1.call-update) | async-done | bytes 1572880 | tf_op jit(solution)/shard_map/all_gather | solution.py:27
  162.0 77.0 %all-gather.6.cloned.1.call-done = bf16[2048,2048]{1,0:T(8,128)(2,1)} async-done(((bf16[128,2048]{1,0:T(8,128)(2,1)}), bf16[2048,2048]{1,0:T(8,128)(2,1)}) %all-gather.6.cloned.1.call-update) | async-done | bytes 8388624 | tf_op jit(solution)/shard_map/all_gather | solution.py:34
  239.0 9.8 %multiply_reduce_fusion = (bf16[2048]{0:T(1024)(128)(2,1)S(1)}, f32[2048,384]{0,1:T(8,128)S(1)}) fusion(f32[2048,768]{0,1:T(8,128)} %convolution_bitcast_fusion, bf16[2048,2048]{1,0:T(8,128)(2,1)} %all-gather.6.cloned.1.call-done, bf16[1,2048,384]{2,1,0:T(8,128)(2,1)} %all-gather.12.cloned.1.call-done), kind=kOutput, calls=%fused_computation.6 | convolution fusion | flops 3226728448 | bytes 19402752 | tf_op jit(solution)/shard_map/dot_general | solution.py:37
  248.7 30.2 %all_gather.23 = bf16[32768]{0:T(1024)(128)(2,1)S(1)} all-gather(bf16[2048]{0:T(1024)(128)(2,1)S(1)} %get-tuple-element.31), channel_id=1, replica_groups=mesh['dp'=2,'node'=2,'local'=8] {'node','local'}, dimensions={0}, use_global_device_ids=true | all-gather | bytes 69632 | tf_op jit(solution)/shard_map/all_gather | solution.py:58
  279.0 0.6 select_reduce_fusion.1
  279.6 29.9 %all_gather.18 = bf16[2048,16]{0,1:T(8,128)(2,1)S(1)} all-gather(bf16[128,16]{0,1:T(8,128)(2,1)S(1)} %get-tuple-element.26), channel_id=1, replica_groups=mesh['dp'=2,'node'=2,'local'=8] {'node','local'}, dimensions={0}, use_global_device_ids=true | all-gather | bytes 69632 | tf_op jit(solution)/shard_map/all_gather | solution.py:32
  309.6 4.0 multiply_convert_fusion.2
  313.6 1.1 copy-done.2
  314.7 0.5 copy-done.3
  315.2 9.1 %convolution_convert_fusion = bf16[2048,2048]{1,0:T(8,128)(2,1)} fusion(bf16[2048,768]{1,0:T(8,128)(2,1)S(1)} %copy-done.6, bf16[2048,384]{0,1:T(8,128)(2,1)S(1)} %get-tuple-element.28, bf16[2048,384]{0,1:T(8,128)(2,1)S(1)} %get-tuple-element.27), kind=kOutput, calls=%fused_computation | convolution fusion | flops 6452936704 | bytes 14680064 | tf_op jit(solution)/shard_map/dot_general | solution.py:50
  324.4 10.2 %fusion.1 = f32[768,2048]{1,0:T(8,128)S(1)} fusion(bf16[2048,2048]{1,0:T(8,128)(2,1)} %all-gather.10.cloned.1.call-done, bf16[2048,384]{0,1:T(8,128)(2,1)} %copy-done.3, bf16[2048,384]{0,1:T(8,128)(2,1)} %copy-done.2), kind=kOutput, calls=%fused_computation.12 | convolution fusion | flops 6448742400 | bytes 17825792 | tf_op jit(solution)/shard_map/dot_general | solution.py:54
  334.5 1.5 fusion.2
  336.1 1.5 collective-permute-start
  337.6 6.8 %fusion.3 = f32[384,2048]{1,0:T(8,128)S(1)} fusion(bf16[2048,2048]{1,0:T(8,128)(2,1)} %all-gather.6.cloned.1.call-done, f32[2048]{0:T(1024)S(1)} %select_reduce_fusion, f32[2048,768]{0,1:T(8,128)S(1)} %bitcast.34), kind=kOutput, calls=%fused_computation.14 | convolution fusion | flops 3226730496 | bytes 17833984 | tf_op jit(solution)/shard_map/dot_general | solution.py:55
  344.4 0.1 fusion.8
  344.5 1.6 copy-done.1
  346.1 1.3 collective-permute-start.1
  347.4 42.4 %collective-permute-done.1 = bf16[1024,384]{0,1:T(8,128)(2,1)S(1)} collective-permute-done((bf16[1024,384]{0,1:T(8,128)(2,1)S(1)}, bf16[1024,384]{0,1:T(8,128)(2,1)S(1)}, u32[]{:S(2)}, u32[]{:S(2)}) %collective-permute-start.1) | collective-permute-done | bytes 786464 | tf_op jit(solution)/shard_map/ppermute | solution.py:92
  389.8 1.7 fusion.4
  391.5 1.6 copy.31
  393.1 2.9 bitcast_add_fusion
  396.0 0.2 slice_bitcast_fusion
  396.3 1.6 copy.30
  397.9 1.6 copy.29
  399.5 27.9 %reduce-scatter.2.cloned.1.call-done = bf16[128,2048]{1,0:T(8,128)(2,1)} async-done(((bf16[2048,2048]{1,0:T(8,128)(2,1)}), bf16[128,2048]{1,0:T(8,128)(2,1)}) %reduce-scatter.2.cloned.1.call-update) | async-done | bytes 524304 | tf_op jit(solution)/shard_map/reduce_scatter | solution.py:53
  (29 shorter events, 0.4 us)
Async XLA Ops:
  7.2 50.6 %all-gather.8.cloned.1.call-start = ((), (), s32[]{:S(2)}) async-start(), calls=%async_computation.2 | async-start | bytes 4718592 | tf_op jit(solution)/shard_map/all_gather | solution.py:24
  7.2 4.8 %copy-start.5 = (bf16[128,8]{0,1:T(8,128)(2,1)S(1)}, bf16[128,8]{0,1:T(8,128)(2,1)}, u32[]{:S(2)}) copy-start(bf16[128,8]{0,1:T(8,128)(2,1)} %param.10) | copy-start | bytes 6148
  9.9 125.0 %all-gather.10.cloned.1.call-start = ((), (), s32[]{:S(2)}) async-start(), calls=%async_computation.3 | async-start | bytes 8912896 | tf_op jit(solution)/shard_map/all_gather | solution.py:33
  10.6 151.3 %all-gather.12.cloned.1.call-start = ((), (), s32[]{:S(2)}) async-start(), calls=%async_computation.5 | async-start | bytes 2359296 | tf_op jit(solution)/shard_map/all_gather | solution.py:27
  11.4 227.6 %all-gather.6.cloned.1.call-start = ((), (), s32[]{:S(2)}) async-start(), calls=%async_computation.1 | async-start | bytes 8912896 | tf_op jit(solution)/shard_map/all_gather | solution.py:34
  12.0 415.5 %reduce-scatter.2.cloned.1.call-start = ((), (), s32[]{:S(2)}) async-start(), calls=%async_computation.4 | async-start | bytes 8912896 | tf_op jit(solution)/shard_map/reduce_scatter | solution.py:53
  146.7 132.3 %copy-start.4 = (s32[128,8]{0,1:T(8,128)S(1)}, s32[128,8]{0,1:T(8,128)}, u32[]{:S(2)}) copy-start(s32[128,8]{0,1:T(8,128)} %param.9) | copy-start | bytes 12292
  309.6 5.7 %copy-start.6 = (bf16[2048,768]{1,0:T(8,128)(2,1)S(1)}, bf16[2048,768]{1,0:T(8,128)(2,1)}, u32[]{:S(2)}) copy-start(bf16[2048,768]{1,0:T(8,128)(2,1)} %all-gather.8.cloned.1.call-done) | copy-start | bytes 9437188
  313.6 1.1 copy-start.2
  313.6 1.7 copy-start.3
  324.3 13.2 %slice-start = ((s8[6291456]{0:T(1024)(128)(4,1)}), s8[2097152]{0:T(1024)(128)(4,1)S(1)}, s32[]{:S(2)}) async-start(s8[6291456]{0:T(1024)(128)(4,1)} %bitcast.33), calls=%async_computation.6 | async-start | bytes 4194304
  324.4 13.2 %slice-start.1 = ((s8[6291456]{0:T(1024)(128)(4,1)}), s8[4194304]{0:T(1024)(128)(4,1)S(1)}, s32[]{:S(2)}) async-start(s8[6291456]{0:T(1024)(128)(4,1)} %bitcast.33), calls=%async_computation.7 | async-start | bytes 8388608
  334.5 9.9 %copy-start = (f32[768,2048]{1,0:T(8,128)}, f32[768,2048]{1,0:T(8,128)S(1)}, u32[]{:S(2)}) copy-start(f32[768,2048]{1,0:T(8,128)S(1)} %fusion.1) | copy-start | bytes 18874372
  336.1 57.1 %collective-permute-start = (bf16[1024,768]{0,1:T(8,128)(2,1)}, bf16[1024,768]{0,1:T(8,128)(2,1)}, u32[]{:S(2)}, u32[]{:S(2)}) collective-permute-start(bf16[1024,768]{0,1:T(8,128)(2,1)} %fusion.2), channel_id=1, source_target_pairs={{0,16},{16,0},{1,17},{17,1},{2,18},{18,2},{3,19},{19,3},{4,20},{20... | collective-permute-start | bytes 4718600 | tf_op jit(solution)/shard_map/ppermute | solution.py:92
  344.4 1.7 copy-start.1
  346.1 43.7 %collective-permute-start.1 = (bf16[1024,384]{0,1:T(8,128)(2,1)S(1)}, bf16[1024,384]{0,1:T(8,128)(2,1)S(1)}, u32[]{:S(2)}, u32[]{:S(2)}) collective-permute-start(bf16[1024,384]{0,1:T(8,128)(2,1)S(1)} %fusion.8), channel_id=1, source_target_pairs={{0,16},{16,0},{1,17},{17,1},{2,18},{18,2},{3,19},{19,3},{4,20},{20... | collective-permute-start | bytes 2359304 | tf_op jit(solution)/shard_map/ppermute | solution.py:92
Sparse Core Ops, SparseCore 0:
  10.1 47.6 all-gather.7
  60.0 74.8 all-gather.9
  136.5 25.4 all-gather.11
  164.0 74.8 all-gather.5
  324.5 102.9 reduce-scatter.1

commit v2 on v1

--- a/solution.py
+++ b/solution.py
@@ -3,7 +3,6 @@
 from jax import lax
 from jax.sharding import PartitionSpec as P
 
-EXPERT_AXES = ("node", "local")
 PIECE_TOKENS = 2048
 
 
@@ -21,17 +20,32 @@
         jnp.where(named, gates.astype(jnp.float32)[:, :, None], 0.0), axis=1
     ).astype(jnp.bfloat16)
 
-    w_in = lax.all_gather(
-        jnp.concatenate([w_gate[0], w_up[0]], axis=1), "dp", axis=0, tiled=True
-    )
-    w_out = lax.all_gather(w_down[0], "dp", axis=0, tiled=True)
-    mine = jnp.arange(experts, dtype=jnp.int32)[None, :] == expert
+    def over_dp(shard):
+        full = jnp.zeros((replicas * half, shard.shape[1]), shard.dtype)
+        full = lax.dynamic_update_slice_in_dim(full, shard, dp * half, axis=0)
+        for shift in range(1, replicas):
+            pairs = [(i, (i + shift) % replicas) for i in range(replicas)]
+            origin = lax.rem(dp + replicas - shift, replicas)
+            full = lax.dynamic_update_slice_in_dim(
+                full, lax.ppermute(shard, "dp", pairs), origin * half, axis=0
+            )
+        return full
+
+    w_in = over_dp(jnp.concatenate([w_gate[0], w_up[0]], axis=1))
+    w_out = over_dp(w_down[0])
+    padded = (experts + 127) // 128 * 128
+    table = jnp.pad(table, ((0, 0), (0, padded - experts)))
+    order = list(range(0, members, 2)) + list(range(members - 1, 0, -2))
+    rightward = [(order[i], order[(i + 1) % members]) for i in range(members)]
+    leftward = [(b, a) for a, b in rightward]
+    right_steps = members // 2
+    left_steps = members - 1 - right_steps
+    groups = lax.axis_size("node")
+
+    mine = jnp.arange(padded, dtype=jnp.int32)[None, :] == expert
     over_rows = (((0,), (0,)), ((), ()))
 
-    def piece(tokens, cotangent, table):
-        all_table = lax.all_gather(table, EXPERT_AXES, axis=0, tiled=True)
-        x = lax.all_gather(tokens, EXPERT_AXES, axis=0, tiled=True)
-        dy = lax.all_gather(cotangent, EXPERT_AXES, axis=0, tiled=True)
+    def work(x, dy, all_table):
         weight = jnp.sum(jnp.where(mine, all_table.astype(jnp.float32), 0.0), axis=1)[:, None]
         pre = jnp.dot(x, w_in, preferred_element_type=jnp.float32)
         upstream = jnp.dot(dy, w_out, preferred_element_type=jnp.float32)
@@ -39,7 +53,8 @@
         sig = jax.nn.sigmoid(pre_gate)
         activated = pre_gate * sig
         hidden = activated * pre_up
-        gate_row = jnp.sum(upstream * hidden, axis=1).astype(jnp.bfloat16)
+        gate_row = jnp.sum(upstream * hidden, axis=1)[:, None]
+        gate_cols = jnp.where(mine, gate_row, 0.0).astype(jnp.bfloat16)
         scaled_hidden = (weight * hidden).astype(jnp.bfloat16)
         hidden_grad = weight * upstream
         gate_part = hidden_grad * pre_up * sig * (1.0 + pre_gate * (1.0 - sig))
@@ -50,17 +65,65 @@
         rows = lax.dot_general(
             pre_grad, w_in, (((1,), (1,)), ((), ())), preferred_element_type=jnp.float32
         ).astype(jnp.bfloat16)
-        input_grad = lax.psum_scatter(rows, EXPERT_AXES, scatter_dimension=0, tiled=True)
         in_grad = lax.dot_general(x, pre_grad, over_rows, preferred_element_type=jnp.float32)
         out_grad = lax.dot_general(
             dy, scaled_hidden, over_rows, preferred_element_type=jnp.float32
         )
-        gate_rows = lax.all_gather(gate_row, EXPERT_AXES, axis=0, tiled=True)
+        return in_grad, out_grad, rows, gate_cols
+
+    def piece(tokens, cotangent, table):
         count = tokens.shape[0]
-        gate_rows = lax.dynamic_slice_in_dim(
-            gate_rows.reshape(experts, experts * count), expert * count, count, axis=1
-        )
-        return in_grad, out_grad, input_grad, gate_rows
+        block = jnp.concatenate([tokens, cotangent, table], axis=1)
+        slots = {0: block}
+        for step in range(1, right_steps + 1):
+            slots[-step] = lax.ppermute(slots[1 - step], "local", rightward)
+            if step <= left_steps:
+                slots[step] = lax.ppermute(slots[step - 1], "local", leftward)
+        near = right_steps // 2
+        halves = [
+            [k for k in slots if abs(k) <= near],
+            [k for k in slots if abs(k) > near],
+        ]
+        in_grad = out_grad = None
+        totals = {}
+        for keys in halves:
+            if not keys:
+                continue
+            blocks = [slots[k] for k in keys]
+            for g in range(1, groups):
+                pairs = [(i, (i + g) % groups) for i in range(groups)]
+                blocks += [lax.ppermute(slots[k], "node", pairs) for k in keys]
+            got = work(
+                jnp.concatenate([b[:, :width] for b in blocks]),
+                jnp.concatenate([b[:, width : 2 * width] for b in blocks]),
+                jnp.concatenate([b[:, 2 * width :] for b in blocks]),
+            )
+            in_grad = got[0] if in_grad is None else in_grad + got[0]
+            out_grad = got[1] if out_grad is None else out_grad + got[1]
+            size = len(keys) * count
+            sums = [part[:size].astype(jnp.float32) for part in got[2:]]
+            for g in range(1, groups):
+                pairs = [(i, (i - g) % groups) for i in range(groups)]
+                for n, part in enumerate(got[2:]):
+                    back = lax.ppermute(part[g * size : (g + 1) * size], "node", pairs)
+                    sums[n] = sums[n] + back.astype(jnp.float32)
+            total = jnp.concatenate(sums, axis=1).astype(jnp.bfloat16)
+            for n, k in enumerate(keys):
+                totals[k] = total[n * count : (n + 1) * count]
+
+        home = totals[0].astype(jnp.float32)
+        for far, sign, pairs in ((right_steps, -1, leftward), (left_steps, 1, rightward)):
+            if far == 0:
+                continue
+            moving = totals[sign * far]
+            for step in range(far, 1, -1):
+                moving = lax.ppermute(moving, "local", pairs).astype(jnp.float32)
+                moving = (moving + totals[sign * (step - 1)].astype(jnp.float32)).astype(
+                    jnp.bfloat16
+                )
+            home = home + lax.ppermute(moving, "local", pairs).astype(jnp.float32)
+        home = home.astype(jnp.bfloat16)
+        return in_grad, out_grad, home[:, :width], home[:, width : width + experts]
 
     pieces = max(1, experts * tokens_dev // PIECE_TOKENS)
     if pieces == 1:
@@ -78,7 +141,7 @@
         cut = [a.reshape(pieces, -1, a.shape[1]) for a in (tokens, cotangent, table)]
         (in_grad, out_grad), (input_grad, by_expert) = lax.scan(step, start, tuple(cut))
         input_grad = input_grad.reshape(tokens_dev, width)
-        by_expert = by_expert.transpose(1, 0, 2).reshape(experts, tokens_dev)
+        by_expert = by_expert.reshape(tokens_dev, experts)
 
     def own(total):
         return lax.dynamic_slice_in_dim(total, dp * half, half, axis=0)
@@ -96,7 +159,7 @@
     out_sum = over_replicas(out_grad)
 
     gate_grad = jnp.sum(
-        jnp.where(named, by_expert.T.astype(jnp.float32)[:, None, :], 0.0), axis=2
+        jnp.where(named, by_expert.astype(jnp.float32)[:, None, :], 0.0), axis=2
     ).astype(jnp.bfloat16)
     return (
         input_grad,

time: 434 us -> 212 us (0.49)
  waiting for transfers between devices: 287 us -> 89.2 us
  blocking collectives: 60.1 us -> 0 us
  local copies, waits for them, and re-layouts: 10 us -> 36 us
  starting transfers between devices: 2.97 us -> 24.6 us
  between operations: 14 us -> 1.05 us
    all_gather x4 -> x0, waiting for transfers between devices: 215 us -> none  [the longest x1 77.1 us: piece(): x = lax.all_gather(tokens, EXPERT_AXES, axis=0, tiled=True)]
    ppermute x0 -> x28, waiting for transfers between devices: none -> 85 us  [the longest x2 31.6 us: over_dp(): lax.ppermute(shard, 'dp', pairs)]
    all_gather x2 -> x0, blocking collectives: 60.1 us -> none  [the longest x1 30.2 us: piece(): gate_rows = lax.all_gather(gate_row, EXPERT_AXES, axis=0, tiled=True)]
    ppermute x2, waiting for transfers between devices: 42.4 us -> 4.17 us  [over_replicas(): lax.ppermute(part.astype(jnp.bfloat16), 'dp', pairs).astype(jnp.float32)]
    reduce_scatter x1 -> x0, waiting for transfers between devices: 27.9 us -> none  [piece(): lax.psum_scatter(rows, EXPERT_AXES, scatter_dimension=0, tiled=True)]
    ppermute x0 -> x28, starting transfers between devices: none -> 21.3 us  [the longest x4 8.52 us: piece(): slots[-step] = lax.ppermute(slots[1 - step], 'local', rightward)]
    unnamed x21 -> x45, local copies, waits for them, and re-layouts: 8.1 us -> 21.9 us
    dynamic_update_slice x0 -> x3, local copies, waits for them, and re-layouts: none -> 6.85 us  [the longest x2 4.76 us: over_dp(): lax.dynamic_update_slice_in_dim(full, lax.ppermute(shard, 'dp', pairs), o...]
  transfers between devices with their start and end apart: 7 -> 30, of which waited for: 6 -> 14; matrix products, arithmetic and copies ran while one was open for 9% -> 42% of each run, Pallas kernels for 0% -> 0%
where the time goes in v2:
time: 212 us; the launch traced here: 211 us
  waiting for transfers between devices  89.2 us (42%)
  matrix products  50 us (24%)
  local copies, waits for them, and re-layouts  36 us (17%)
  starting transfers between devices  24.6 us (12%)
  other arithmetic  9.93 us (5%)
    ppermute x2, waiting for transfers between devices, over_dp(): lax.ppermute(shard, 'dp', pairs)  31.6 us
    ppermute x5, waiting for transfers between devices, piece(): moving = lax.ppermute(moving, 'local', pairs).astype(jnp.float32)  28.9 us
    unnamed x45, local copies, waits for them, and re-layouts  21.9 us
    ppermute x4, waiting for transfers between devices, piece(): slots[-step] = lax.ppermute(slots[1 - step], 'local', rightward)  17.3 us
    dot_general x2, matrix products, work(): pre = jnp.dot(x, w_in, preferred_element_type=jnp.float32)  12.6 us
    dot_general x2, matrix products, work(): lax.dot_general(pre_grad, w_in, (((1,), (1,)), ((), ())), preferred_eleme...  12.1 us
    dot_general x2, matrix products, work(): lax.dot_general(x, pre_grad, over_rows, preferred_element_type=jnp.float32)  11.1 us
    dot_general x2, matrix products, work(): upstream = jnp.dot(dy, w_out, preferred_element_type=jnp.float32)  9.28 us
  transfers between devices with their start and end apart: 30, of which 14 were waited for; matrix products, arithmetic and copies ran while one was open for 42% of the time, Pallas kernels for 0%

profile of v2, /device:TPU:0, one launch (start us, length us, event | category | flops | bytes accessed | tf_op | source)
XLA Modules:
  0.0 210.9 jit_solution(7273876911025871279)
XLA Ops:
  6.3 3.0 %collective-permute-start = (bf16[128,4224]{0,1:T(8,128)(2,1)}, bf16[128,4224]{0,1:T(8,128)(2,1)}, u32[]{:S(2)}, u32[]{:S(2)}) collective-permute-start(bf16[128,4224]{0,1:T(8,128)(2,1)} %pad_maximum_fusion.5), channel_id=1, source_target_pairs={{0,2},{2,4},{4,6},{6,7},{7,5},{5,3},{3,1},{1,0},{8,10},{10,12},{12... | collective-permute-start | bytes 3244040 | tf_op jit(solution)/shard_map/ppermute | solution.py:79
  9.4 1.9 collective-permute-start.9
  11.3 1.8 broadcast_in_dim.107
  13.2 2.5 %pad_maximum_fusion.1 = (bf16[1024,768]{1,0:T(8,128)(2,1)S(1)}, bf16[2048,768]{1,0:T(8,128)(2,1)}) fusion(bf16[1024,384]{1,0:T(8,128)(2,1)S(1)} %bitcast.24, bf16[1024,384]{1,0:T(8,128)(2,1)} %bitcast.25, bf16[2048,768]{1,0:T(8,128)(2,1)} %broadcast_in_dim.107, s32[]{:T(128)S(6)} %select_n.38), kind=kLoop, calls=%fused_computation.28 | loop fusion | flops 3145728 | bytes 4718596 | tf_op jit(solution)/shard_map/concatenate | solution.py:34
  18.1 2.1 constant_dynamic-update-slice_fusion.21
  20.2 9.9 %collective-permute-done.9 = bf16[1024,384]{1,0:T(8,128)(2,1)} collective-permute-done((bf16[1024,384]{1,0:T(8,128)(2,1)}, bf16[1024,384]{1,0:T(8,128)(2,1)}, u32[]{:S(2)}, u32[]{:S(2)}) %collective-permute-start.9) | collective-permute-done | bytes 786464 | tf_op jit(solution)/shard_map/ppermute | solution.py:30
  30.1 2.1 constant_dynamic-update-slice_fusion.20
  37.0 2.4 %slice_dynamic-update-slice_fusion.20 = (bf16[1280,2048]{0,1:T(8,128)(2,1)}, bf16[1280,2048]{0,1:T(8,128)(2,1)}) fusion(bf16[1280,2048]{0,1:T(8,128)(2,1)} %get-tuple-element.59, bf16[128,4224]{0,1:T(8,128)(2,1)} %collective-permute-done, bf16[1280,2048]{0,1:T(8,128)(2,1)} %get-tuple-element.58), kind=kLoop, calls=%fused_computation.82 | loop fusion | bytes 2097152
  39.4 2.4 %slice_dynamic-update-slice_fusion.19 = (bf16[1280,2048]{0,1:T(8,128)(2,1)}, bf16[1280,2048]{0,1:T(8,128)(2,1)}) fusion(bf16[1280,2048]{0,1:T(8,128)(2,1)} %get-tuple-element.42, bf16[128,4224]{0,1:T(8,128)(2,1)} %collective-permute-done.1, bf16[1280,2048]{0,1:T(8,128)(2,1)} %get-tuple-element.43), kind=kLoop, calls=%fused_computation.81 | loop fusion | bytes 2097152
  41.8 21.7 %collective-permute-done.10 = bf16[1024,768]{1,0:T(8,128)(2,1)} collective-permute-done((bf16[1024,768]{1,0:T(8,128)(2,1)S(1)}, bf16[1024,768]{1,0:T(8,128)(2,1)}, u32[]{:S(2)}, u32[]{:S(2)}) %collective-permute-start.10) | collective-permute-done | bytes 1572896 | tf_op jit(solution)/shard_map/ppermute | solution.py:30
  63.5 2.7 %constant_dynamic-update-slice_fusion.18 = bf16[2048,768]{1,0:T(8,128)(2,1)} fusion(bf16[2048,768]{1,0:T(8,128)(2,1)} %get-tuple-element.25, bf16[1024,768]{1,0:T(8,128)(2,1)} %collective-permute-done.10, s32[]{:T(128)S(6)} %select_n.39), kind=kLoop, calls=%fused_computation.118 | loop fusion | bytes 3145732 | tf_op jit(solution)/shard_map/dynamic_update_slice | solution.py:29
  66.8 1.9 collective-permute-start.13
  72.0 2.3 %slice_dynamic-update-slice_fusion.16 = (bf16[1280,2048]{0,1:T(8,128)(2,1)}, bf16[1280,2048]{0,1:T(8,128)(2,1)}) fusion(bf16[1280,2048]{0,1:T(8,128)(2,1)} %get-tuple-element.36, bf16[128,4224]{0,1:T(8,128)(2,1)} %collective-permute-done.4, bf16[1280,2048]{0,1:T(8,128)(2,1)} %get-tuple-element.37), kind=kLoop, calls=%fused_computation.78 | loop fusion | bytes 2097152
  78.9 7.9 %fusion.18 = f32[1280,768]{0,1:T(8,128)S(1)} fusion(bf16[1280,2048]{0,1:T(8,128)(2,1)} %get-tuple-element.26, bf16[2048,768]{1,0:T(8,128)(2,1)} %constant_dynamic-update-slice_fusion.18), kind=kOutput, calls=%fused_computation.127 | convolution fusion | flops 4026531840 | bytes 12320768 | tf_op jit(solution)/shard_map/dot_general | solution.py:50
  87.0 5.9 %multiply_convert_fusion.2 = (bf16[1280,384]{0,1:T(8,128)(2,1)S(1)}, bf16[1280,384]{0,1:T(8,128)(2,1)S(1)}, bf16[1280]{0:T(1024)(128)(2,1)S(1)}) fusion(f32[1280,768]{0,1:T(8,128)S(1)} %fusion.18, f32[1280]{0:T(1024)S(1)} %select_reduce_fusion, bf16[1280,2048]{0,1:T(8,128)(2,1)S(1)} %copy-done.2, bf16[2048,384]{1,0:T(8,128)(2,1)} %constant_dynamic-update-slice_fusion.20), kind=kOutput, calls=%fused_computation.22 | convolution fusion | flops 2021620480 | bytes 12721664 | tf_op jit(solution)/shard_map/dot_general | solution.py:51
  93.2 6.2 %fusion.1 = f32[2048,768]{1,0:T(8,128)} fusion(bf16[1280,2048]{0,1:T(8,128)(2,1)S(1)} %copy-done.3, bf16[1280,384]{0,1:T(8,128)(2,1)S(1)} %get-tuple-element.11, bf16[1280,384]{0,1:T(8,128)(2,1)S(1)} %get-tuple-element.10), kind=kOutput, calls=%fused_computation.33 | convolution fusion | flops 4030464000 | bytes 13500416 | tf_op jit(solution)/shard_map/dot_general | solution.py:68
  101.2 7.4 %convolution_convert_fusion = bf16[1280,2048]{0,1:T(8,128)(2,1)S(1)} fusion(bf16[2048,768]{1,0:T(8,128)(2,1)} %constant_dynamic-update-slice_fusion.18, bf16[1280,384]{0,1:T(8,128)(2,1)S(1)} %get-tuple-element.11, bf16[1280,384]{0,1:T(8,128)(2,1)S(1)} %get-tuple-element.10), kind=kOutput, calls=%fused_computation | convolution fusion | flops 4033085440 | bytes 10354688 | tf_op jit(solution)/shard_map/dot_general | solution.py:65
  109.7 16.0 %collective-permute-done.15 = bf16[128,4224]{0,1:T(8,128)(2,1)S(1)} collective-permute-done((bf16[128,4224]{0,1:T(8,128)(2,1)S(1)}, bf16[128,4224]{0,1:T(8,128)(2,1)S(1)}, u32[]{:S(2)}, u32[]{:S(2)}) %collective-permute-start.15) | collective-permute-done | bytes 1081376 | tf_op jit(solution)/shard_map/ppermute | solution.py:79
  126.5 1.9 collective-permute-done.18
  128.6 4.8 %fusion.19 = f32[768,768]{0,1:T(8,128)S(1)} fusion(bf16[768,2048]{0,1:T(8,128)(2,1)S(1)} %get-tuple-element.44, bf16[2048,768]{1,0:T(8,128)(2,1)} %constant_dynamic-update-slice_fusion.18), kind=kOutput, calls=%fused_computation.128 | convolution fusion | flops 2415919104 | bytes 8650752 | tf_op jit(solution)/shard_map/dot_general | solution.py:50
  133.5 3.4 %multiply_convert_fusion.5 = (bf16[768,384]{0,1:T(8,128)(2,1)S(1)}, bf16[768,384]{0,1:T(8,128)(2,1)S(1)}, bf16[768]{0:T(1024)(128)(2,1)S(1)}) fusion(f32[768,768]{0,1:T(8,128)S(1)} %fusion.19, f32[768]{0:T(1024)S(1)} %select_reduce_fusion.1, bf16[768,2048]{0,1:T(8,128)(2,1)S(1)} %get-tuple-element.45, bf16[2048,384]{1,0:T(8,128)(2,1)} %constant_dynamic-update-slice_fusion.20), kind=kOutput, calls=%fused_computation.38 | convolution fusion | flops 1212972288 | bytes 8262144 | tf_op jit(solution)/shard_map/dot_general | solution.py:51
  136.9 4.7 %convolution_convert_fusion.1 = bf16[768,2048]{0,1:T(8,128)(2,1)S(1)} fusion(bf16[2048,768]{1,0:T(8,128)(2,1)} %constant_dynamic-update-slice_fusion.18, bf16[768,384]{0,1:T(8,128)(2,1)S(1)} %get-tuple-element.14, bf16[768,384]{0,1:T(8,128)(2,1)S(1)} %get-tuple-element.13), kind=kOutput, calls=%fused_computation.7 | convolution fusion | flops 2419851264 | bytes 7471104 | tf_op jit(solution)/shard_map/dot_general | solution.py:65
  141.9 3.0 %fusion.3 = f32[2048,384]{1,0:T(8,128)S(1)} fusion(bf16[1280,2048]{0,1:T(8,128)(2,1)S(1)} %copy-done.2, f32[1280]{0:T(1024)S(1)} %select_reduce_fusion, f32[1280,768]{0,1:T(8,128)S(1)} %copy-done.6), kind=kOutput, calls=%fused_computation.49 | convolution fusion | flops 2016706560 | bytes 12325888 | tf_op jit(solution)/shard_map/dot_general | solution.py:69
  146.3 2.0 convolution_add_fusion.1
  153.0 4.9 %convolution_add_fusion = f32[2048,768]{1,0:T(8,128)S(1)} fusion(f32[2048,768]{1,0:T(8,128)} %fusion.1, bf16[768,2048]{0,1:T(8,128)(2,1)S(1)} %get-tuple-element.44, bf16[768,384]{0,1:T(8,128)(2,1)S(1)} %get-tuple-element.14, bf16[768,384]{0,1:T(8,128)(2,1)S(1)} %get-tuple-element.13), kind=kOutput, calls=%fused_computation.6 | convolution fusion | flops 2419851264 | bytes 16908288 | tf_op jit(solution)/shard_map/dot_general | solution.py:68
  160.1 6.1 %collective-permute-done.21 = bf16[128,2176]{0,1:T(8,128)(2,1)S(1)} collective-permute-done((bf16[128,2176]{0,1:T(8,128)(2,1)S(1)}, bf16[128,2176]{0,1:T(8,128)(2,1)S(1)}, u32[]{:S(2)}, u32[]{:S(2)}) %collective-permute-start.21) | collective-permute-done | bytes 557088 | tf_op jit(solution)/shard_map/ppermute | solution.py:120
  168.8 5.1 %collective-permute-done.25 = bf16[128,2176]{0,1:T(8,128)(2,1)S(1)} collective-permute-done((bf16[128,2176]{0,1:T(8,128)(2,1)S(1)}, bf16[128,2176]{0,1:T(8,128)(2,1)S(1)}, u32[]{:S(2)}, u32[]{:S(2)}) %collective-permute-start.25) | collective-permute-done | bytes 557088 | tf_op jit(solution)/shard_map/ppermute | solution.py:120
  173.9 6.6 %collective-permute-done.22 = bf16[128,2176]{0,1:T(8,128)(2,1)S(1)} collective-permute-done((bf16[128,2176]{0,1:T(8,128)(2,1)S(1)}, bf16[128,2176]{0,1:T(8,128)(2,1)S(1)}, u32[]{:S(2)}, u32[]{:S(2)}) %collective-permute-start.22) | collective-permute-done | bytes 557088 | tf_op jit(solution)/shard_map/ppermute | solution.py:120
  184.2 9.9 %collective-permute-done.23 = bf16[128,2176]{0,1:T(8,128)(2,1)S(1)} collective-permute-done((bf16[128,2176]{0,1:T(8,128)(2,1)S(1)}, bf16[128,2176]{0,1:T(8,128)(2,1)S(1)}, u32[]{:S(2)}, u32[]{:S(2)}) %collective-permute-start.23) | collective-permute-done | bytes 557088 | tf_op jit(solution)/shard_map/ppermute | solution.py:120
  197.8 4.2 %collective-permute-done.28 = bf16[1024,768]{1,0:T(8,128)(2,1)S(1)} collective-permute-done((bf16[1024,768]{1,0:T(8,128)(2,1)S(1)}, bf16[1024,768]{1,0:T(8,128)(2,1)S(1)}, u32[]{:S(2)}, u32[]{:S(2)}) %collective-permute-start.28) | collective-permute-done | bytes 1572896 | tf_op jit(solution)/shard_map/ppermute | solution.py:155
  202.3 1.9 slice_bitcast_fusion
  204.1 3.6 %collective-permute-done.24 = bf16[128,2176]{0,1:T(8,128)(2,1)S(1)} collective-permute-done((bf16[128,2176]{0,1:T(8,128)(2,1)S(1)}, bf16[128,2176]{0,1:T(8,128)(2,1)S(1)}, u32[]{:S(2)}, u32[]{:S(2)}) %collective-permute-start.24) | collective-permute-done | bytes 557088 | tf_op jit(solution)/shard_map/ppermute | solution.py:124
  (122 shorter events, 47.9 us)
Async XLA Ops:
  6.3 27.1 %collective-permute-start = (bf16[128,4224]{0,1:T(8,128)(2,1)}, bf16[128,4224]{0,1:T(8,128)(2,1)}, u32[]{:S(2)}, u32[]{:S(2)}) collective-permute-start(bf16[128,4224]{0,1:T(8,128)(2,1)} %pad_maximum_fusion.5), channel_id=1, source_target_pairs={{0,2},{2,4},{4,6},{6,7},{7,5},{5,3},{3,1},{1,0},{8,10},{10,12},{12... | collective-permute-start | bytes 3244040 | tf_op jit(solution)/shard_map/ppermute | solution.py:79
  9.4 25.9 %collective-permute-start.1 = (bf16[128,4224]{0,1:T(8,128)(2,1)}, bf16[128,4224]{0,1:T(8,128)(2,1)}, u32[]{:S(2)}, u32[]{:S(2)}) collective-permute-start(bf16[128,4224]{0,1:T(8,128)(2,1)} %pad_maximum_fusion.5), channel_id=1, source_target_pairs={{2,0},{4,2},{6,4},{7,6},{5,7},{3,5},{1,3},{0,1},{10,8},{12,10},{14... | collective-permute-start | bytes 3244040 | tf_op jit(solution)/shard_map/ppermute | solution.py:81
  9.4 57.5 %collective-permute-start.4 = (bf16[128,4224]{0,1:T(8,128)(2,1)}, bf16[128,4224]{0,1:T(8,128)(2,1)}, u32[]{:S(2)}, u32[]{:S(2)}) collective-permute-start(bf16[128,4224]{0,1:T(8,128)(2,1)} %pad_maximum_fusion.5), channel_id=1, source_target_pairs={{0,8},{8,0},{1,9},{9,1},{2,10},{10,2},{3,11},{11,3},{4,12},{12,4},... | collective-permute-start | bytes 3244040 | tf_op jit(solution)/shard_map/ppermute | solution.py:95
  9.4 20.7 %collective-permute-start.9 = (bf16[1024,384]{1,0:T(8,128)(2,1)}, bf16[1024,384]{1,0:T(8,128)(2,1)}, u32[]{:S(2)}, u32[]{:S(2)}) collective-permute-start(bf16[1024,384]{1,0:T(8,128)(2,1)} %bitcast), channel_id=1, source_target_pairs={{0,16},{16,0},{1,17},{17,1},{2,18},{18,2},{3,19},{19,3},{4,20},{20... | collective-permute-start | bytes 2359304 | tf_op jit(solution)/shard_map/ppermute | solution.py:30
  15.7 47.9 %collective-permute-start.10 = (bf16[1024,768]{1,0:T(8,128)(2,1)S(1)}, bf16[1024,768]{1,0:T(8,128)(2,1)}, u32[]{:S(2)}, u32[]{:S(2)}) collective-permute-start(bf16[1024,768]{1,0:T(8,128)(2,1)S(1)} %get-tuple-element.24), channel_id=1, source_target_pairs={{0,16},{16,0},{1,17},{17,1},{2,18},{18,2},{3,19},{19,3},{4,20},{20... | collective-permute-start | bytes 4718600 | tf_op jit(solution)/shard_map/ppermute | solution.py:30
  16.9 18.7 %copy-start.1 = (bf16[1280,128]{0,1:T(8,128)(2,1)S(1)}, bf16[1280,128]{0,1:T(8,128)(2,1)}, u32[]{:S(2)}) copy-start(bf16[1280,128]{0,1:T(8,128)(2,1)} %get-tuple-element.56) | copy-start | bytes 983044
  33.5 32.7 %collective-permute-start.2 = (bf16[128,4224]{0,1:T(8,128)(2,1)}, bf16[128,4224]{0,1:T(8,128)(2,1)S(1)}, u32[]{:S(2)}, u32[]{:S(2)}) collective-permute-start(bf16[128,4224]{0,1:T(8,128)(2,1)} %collective-permute-done), channel_id=1, source_target_pairs={{0,2},{2,4},{4,6},{6,7},{7,5},{5,3},{3,1},{1,0},{8,10},{10,12},{12... | collective-permute-start | bytes 3244040 | tf_op jit(solution)/shard_map/ppermute | solution.py:79
  35.3 36.6 %collective-permute-start.5 = (bf16[128,4224]{0,1:T(8,128)(2,1)}, bf16[128,4224]{0,1:T(8,128)(2,1)S(1)}, u32[]{:S(2)}, u32[]{:S(2)}) collective-permute-start(bf16[128,4224]{0,1:T(8,128)(2,1)} %collective-permute-done), channel_id=1, source_target_pairs={{0,8},{8,0},{1,9},{9,1},{2,10},{10,2},{3,11},{11,3},{4,12},{12,4},... | collective-permute-start | bytes 3244040 | tf_op jit(solution)/shard_map/ppermute | solution.py:95
  35.3 31.4 %collective-permute-start.3 = (bf16[128,4224]{0,1:T(8,128)(2,1)}, bf16[128,4224]{0,1:T(8,128)(2,1)S(1)}, u32[]{:S(2)}, u32[]{:S(2)}) collective-permute-start(bf16[128,4224]{0,1:T(8,128)(2,1)} %collective-permute-done.1), channel_id=1, source_target_pairs={{2,0},{4,2},{6,4},{7,6},{5,7},{3,5},{1,3},{0,1},{10,8},{12,10},{14... | collective-permute-start | bytes 3244040 | tf_op jit(solution)/shard_map/ppermute | solution.py:81
  63.5 12.0 %collective-permute-start.6 = (bf16[128,4224]{0,1:T(8,128)(2,1)}, bf16[128,4224]{0,1:T(8,128)(2,1)S(1)}, u32[]{:S(2)}, u32[]{:S(2)}) collective-permute-start(bf16[128,4224]{0,1:T(8,128)(2,1)} %collective-permute-done.1), channel_id=1, source_target_pairs={{0,8},{8,0},{1,9},{9,1},{2,10},{10,2},{3,11},{11,3},{4,12},{12,4},... | collective-permute-start | bytes 3244040 | tf_op jit(solution)/shard_map/ppermute | solution.py:95
  66.2 10.4 %collective-permute-start.7 = (bf16[128,4224]{0,1:T(8,128)(2,1)S(1)}, bf16[128,4224]{0,1:T(8,128)(2,1)S(1)}, u32[]{:S(2)}, u32[]{:S(2)}) collective-permute-start(bf16[128,4224]{0,1:T(8,128)(2,1)S(1)} %collective-permute-done.2), channel_id=1, source_target_pairs={{0,8},{8,0},{1,9},{9,1},{2,10},{10,2},{3,11},{11,3},{4,12},{12,4},... | collective-permute-start | bytes 3244040 | tf_op jit(solution)/shard_map/ppermute | solution.py:95
  66.7 11.1 %collective-permute-start.8 = (bf16[128,4224]{0,1:T(8,128)(2,1)S(1)}, bf16[128,4224]{0,1:T(8,128)(2,1)S(1)}, u32[]{:S(2)}, u32[]{:S(2)}) collective-permute-start(bf16[128,4224]{0,1:T(8,128)(2,1)S(1)} %collective-permute-done.3), channel_id=1, source_target_pairs={{0,8},{8,0},{1,9},{9,1},{2,10},{10,2},{3,11},{11,3},{4,12},{12,4},... | collective-permute-start | bytes 3244040 | tf_op jit(solution)/shard_map/ppermute | solution.py:95
  66.8 32.6 %collective-permute-start.13 = (bf16[128,4224]{0,1:T(8,128)(2,1)S(1)}, bf16[128,4224]{0,1:T(8,128)(2,1)S(1)}, u32[]{:S(2)}, u32[]{:S(2)}) collective-permute-start(bf16[128,4224]{0,1:T(8,128)(2,1)S(1)} %collective-permute-done.2), channel_id=1, source_target_pairs={{0,2},{2,4},{4,6},{6,7},{7,5},{5,3},{3,1},{1,0},{8,10},{10,12},{12... | collective-permute-start | bytes 3244040 | tf_op jit(solution)/shard_map/ppermute | solution.py:79
  71.8 37.2 %collective-permute-start.14 = (bf16[128,4224]{0,1:T(8,128)(2,1)S(1)}, bf16[128,4224]{0,1:T(8,128)(2,1)S(1)}, u32[]{:S(2)}, u32[]{:S(2)}) collective-permute-start(bf16[128,4224]{0,1:T(8,128)(2,1)S(1)} %collective-permute-done.3), channel_id=1, source_target_pairs={{2,0},{4,2},{6,4},{7,6},{5,7},{3,5},{1,3},{0,1},{10,8},{12,10},{14... | collective-permute-start | bytes 3244040 | tf_op jit(solution)/shard_map/ppermute | solution.py:81
  78.9 8.1 %copy-start.2 = (bf16[1280,2048]{0,1:T(8,128)(2,1)S(1)}, bf16[1280,2048]{0,1:T(8,128)(2,1)}, u32[]{:S(2)}) copy-start(bf16[1280,2048]{0,1:T(8,128)(2,1)} %get-tuple-element.27) | copy-start | bytes 15728644
  93.1 52.8 %collective-permute-start.12 = (bf16[640,128]{0,1:T(8,128)(2,1)S(1)}, bf16[640,128]{0,1:T(8,128)(2,1)S(1)}, u32[]{:S(2)}, u32[]{:S(2)}) collective-permute-start(bf16[640,128]{0,1:T(8,128)(2,1)S(1)} %slice.308), channel_id=1, source_target_pairs={{0,8},{8,0},{1,9},{9,1},{2,10},{10,2},{3,11},{11,3},{4,12},{12,4},... | collective-permute-start | bytes 491528 | tf_op jit(solution)/shard_map/ppermute | solution.py:108
  99.4 26.3 %collective-permute-start.15 = (bf16[128,4224]{0,1:T(8,128)(2,1)S(1)}, bf16[128,4224]{0,1:T(8,128)(2,1)S(1)}, u32[]{:S(2)}, u32[]{:S(2)}) collective-permute-start(bf16[128,4224]{0,1:T(8,128)(2,1)S(1)} %collective-permute-done.13), channel_id=1, source_target_pairs={{0,2},{2,4},{4,6},{6,7},{7,5},{5,3},{3,1},{1,0},{8,10},{10,12},{12... | collective-permute-start | bytes 3244040 | tf_op jit(solution)/shard_map/ppermute | solution.py:79
  108.8 16.9 %collective-permute-start.16 = (bf16[128,4224]{0,1:T(8,128)(2,1)S(1)}, bf16[128,4224]{0,1:T(8,128)(2,1)S(1)}, u32[]{:S(2)}, u32[]{:S(2)}) collective-permute-start(bf16[128,4224]{0,1:T(8,128)(2,1)S(1)} %collective-permute-done.13), channel_id=1, source_target_pairs={{0,8},{8,0},{1,9},{9,1},{2,10},{10,2},{3,11},{11,3},{4,12},{12,4},... | collective-permute-start | bytes 3244040 | tf_op jit(solution)/shard_map/ppermute | solution.py:95
  109.1 16.9 %collective-permute-start.17 = (bf16[128,4224]{0,1:T(8,128)(2,1)S(1)}, bf16[128,4224]{0,1:T(8,128)(2,1)S(1)}, u32[]{:S(2)}, u32[]{:S(2)}) collective-permute-start(bf16[128,4224]{0,1:T(8,128)(2,1)S(1)} %collective-permute-done.14), channel_id=1, source_target_pairs={{0,8},{8,0},{1,9},{9,1},{2,10},{10,2},{3,11},{11,3},{4,12},{12,4},... | collective-permute-start | bytes 3244040 | tf_op jit(solution)/shard_map/ppermute | solution.py:95
  125.7 2.7 %collective-permute-start.18 = (bf16[128,4224]{0,1:T(8,128)(2,1)S(1)}, bf16[128,4224]{0,1:T(8,128)(2,1)S(1)}, u32[]{:S(2)}, u32[]{:S(2)}) collective-permute-start(bf16[128,4224]{0,1:T(8,128)(2,1)S(1)} %collective-permute-done.15), channel_id=1, source_target_pairs={{0,8},{8,0},{1,9},{9,1},{2,10},{10,2},{3,11},{11,3},{4,12},{12,4},... | collective-permute-start | bytes 3244040 | tf_op jit(solution)/shard_map/ppermute | solution.py:95
  141.7 8.9 %collective-permute-start.19 = (bf16[384,2048]{0,1:T(8,128)(2,1)S(1)}, bf16[384,2048]{0,1:T(8,128)(2,1)S(1)}, u32[]{:S(2)}, u32[]{:S(2)}) collective-permute-start(bf16[384,2048]{0,1:T(8,128)(2,1)S(1)} %slice.332), channel_id=1, source_target_pairs={{0,8},{8,0},{1,9},{9,1},{2,10},{10,2},{3,11},{11,3},{4,12},{12,4},... | collective-permute-start | bytes 4718600 | tf_op jit(solution)/shard_map/ppermute | solution.py:108
  145.5 22.6 %collective-permute-start.11 = (bf16[640,2048]{0,1:T(8,128)(2,1)S(1)}, bf16[640,2048]{0,1:T(8,128)(2,1)S(1)}, u32[]{:S(2)}, u32[]{:S(2)}) collective-permute-start(bf16[640,2048]{0,1:T(8,128)(2,1)S(1)} %slice.306), channel_id=1, source_target_pairs={{0,8},{8,0},{1,9},{9,1},{2,10},{10,2},{3,11},{11,3},{4,12},{12,4},... | collective-permute-start | bytes 7864328 | tf_op jit(solution)/shard_map/ppermute | solution.py:108
  146.1 4.5 %collective-permute-start.20 = (bf16[384,128]{0,1:T(8,128)(2,1)S(1)}, bf16[384,128]{0,1:T(8,128)(2,1)S(1)}, u32[]{:S(2)}, u32[]{:S(2)}) collective-permute-start(bf16[384,128]{0,1:T(8,128)(2,1)S(1)} %slice.334), channel_id=1, source_target_pairs={{0,8},{8,0},{1,9},{9,1},{2,10},{10,2},{3,11},{11,3},{4,12},{12,4},... | collective-permute-start | bytes 294920 | tf_op jit(solution)/shard_map/ppermute | solution.py:108
  148.4 34.5 %collective-permute-start.29 = (bf16[1024,384]{1,0:T(8,128)(2,1)S(1)}, bf16[1024,384]{1,0:T(8,128)(2,1)S(1)}, u32[]{:S(2)}, u32[]{:S(2)}) collective-permute-start(bf16[1024,384]{1,0:T(8,128)(2,1)S(1)} %dynamic-slice_convert_fusion.1), channel_id=1, source_target_pairs={{0,16},{16,0},{1,17},{17,1},{2,18},{18,2},{3,19},{19,3},{4,20},{20... | collective-permute-start | bytes 2359304 | tf_op jit(solution)/shard_map/ppermute | solution.py:155
  151.2 15.0 %collective-permute-start.21 = (bf16[128,2176]{0,1:T(8,128)(2,1)S(1)}, bf16[128,2176]{0,1:T(8,128)(2,1)S(1)}, u32[]{:S(2)}, u32[]{:S(2)}) collective-permute-start(bf16[128,2176]{0,1:T(8,128)(2,1)S(1)} %get-tuple-element.22), channel_id=1, source_target_pairs={{2,0},{4,2},{6,4},{7,6},{5,7},{3,5},{1,3},{0,1},{10,8},{12,10},{14... | collective-permute-start | bytes 1671176 | tf_op jit(solution)/shard_map/ppermute | solution.py:120
  158.0 43.9 %collective-permute-start.28 = (bf16[1024,768]{1,0:T(8,128)(2,1)S(1)}, bf16[1024,768]{1,0:T(8,128)(2,1)S(1)}, u32[]{:S(2)}, u32[]{:S(2)}) collective-permute-start(bf16[1024,768]{1,0:T(8,128)(2,1)S(1)} %dynamic-slice_convert_fusion), channel_id=1, source_target_pairs={{0,16},{16,0},{1,17},{17,1},{2,18},{18,2},{3,19},{19,3},{4,20},{20... | collective-permute-start | bytes 4718600 | tf_op jit(solution)/shard_map/ppermute | solution.py:155
  159.6 14.3 %collective-permute-start.25 = (bf16[128,2176]{0,1:T(8,128)(2,1)S(1)}, bf16[128,2176]{0,1:T(8,128)(2,1)S(1)}, u32[]{:S(2)}, u32[]{:S(2)}) collective-permute-start(bf16[128,2176]{0,1:T(8,128)(2,1)S(1)} %get-tuple-element.23), channel_id=1, source_target_pairs={{0,2},{2,4},{4,6},{6,7},{7,5},{5,3},{3,1},{1,0},{8,10},{10,12},{12... | collective-permute-start | bytes 1671176 | tf_op jit(solution)/shard_map/ppermute | solution.py:120
  166.3 14.2 %collective-permute-start.22 = (bf16[128,2176]{0,1:T(8,128)(2,1)S(1)}, bf16[128,2176]{0,1:T(8,128)(2,1)S(1)}, u32[]{:S(2)}, u32[]{:S(2)}) collective-permute-start(bf16[128,2176]{0,1:T(8,128)(2,1)S(1)} %add_convert_fusion.7), channel_id=1, source_target_pairs={{2,0},{4,2},{6,4},{7,6},{5,7},{3,5},{1,3},{0,1},{10,8},{12,10},{14... | collective-permute-start | bytes 1671176 | tf_op jit(solution)/shard_map/ppermute | solution.py:120
  180.8 13.3 %collective-permute-start.23 = (bf16[128,2176]{0,1:T(8,128)(2,1)S(1)}, bf16[128,2176]{0,1:T(8,128)(2,1)S(1)}, u32[]{:S(2)}, u32[]{:S(2)}) collective-permute-start(bf16[128,2176]{0,1:T(8,128)(2,1)S(1)} %get-tuple-element.20), channel_id=1, source_target_pairs={{2,0},{4,2},{6,4},{7,6},{5,7},{3,5},{1,3},{0,1},{10,8},{12,10},{14... | collective-permute-start | bytes 1671176 | tf_op jit(solution)/shard_map/ppermute | solution.py:120
  182.5 12.9 %collective-permute-start.26 = (bf16[128,2176]{0,1:T(8,128)(2,1)S(1)}, bf16[128,2176]{0,1:T(8,128)(2,1)S(1)}, u32[]{:S(2)}, u32[]{:S(2)}) collective-permute-start(bf16[128,2176]{0,1:T(8,128)(2,1)S(1)} %get-tuple-element.21), channel_id=1, source_target_pairs={{0,2},{2,4},{4,6},{6,7},{7,5},{5,3},{3,1},{1,0},{8,10},{10,12},{12... | collective-permute-start | bytes 1671176 | tf_op jit(solution)/shard_map/ppermute | solution.py:120
  195.7 12.0 %collective-permute-start.24 = (bf16[128,2176]{0,1:T(8,128)(2,1)S(1)}, bf16[128,2176]{0,1:T(8,128)(2,1)S(1)}, u32[]{:S(2)}, u32[]{:S(2)}) collective-permute-start(bf16[128,2176]{0,1:T(8,128)(2,1)S(1)} %get-tuple-element.18), channel_id=1, source_target_pairs={{2,0},{4,2},{6,4},{7,6},{5,7},{3,5},{1,3},{0,1},{10,8},{12,10},{14... | collective-permute-start | bytes 1671176 | tf_op jit(solution)/shard_map/ppermute | solution.py:124
  197.3 11.7 %collective-permute-start.27 = (bf16[128,2176]{0,1:T(8,128)(2,1)S(1)}, bf16[128,2176]{0,1:T(8,128)(2,1)S(1)}, u32[]{:S(2)}, u32[]{:S(2)}) collective-permute-start(bf16[128,2176]{0,1:T(8,128)(2,1)S(1)} %get-tuple-element.19), channel_id=1, source_target_pairs={{0,2},{2,4},{4,6},{6,7},{7,5},{5,3},{3,1},{1,0},{8,10},{10,12},{12... | collective-permute-start | bytes 1671176 | tf_op jit(solution)/shard_map/ppermute | solution.py:124
  (5 other events, 31.4 us)
